TPU v7x, 32 devices: a whole 2x2x4 slice. The times are simulated.
32 devices in a mesh: req: 4 (over y, x), tile: 4 (over z), col: 2 (over core).
Axes of the slice: x: 2, y: 2, z: 4, core: 2. Of those that a mesh axis runs over, the one named last changes fastest.
Arguments:
- img_qkv: bfloat16 [4, 64, 64, 3, 1536], P('req', 'tile', None, None, 'col'), may hold values from -10 to 10
- txt_kv: bfloat16 [4, 512, 2, 1536], P('req', 'tile', None, 'col'), may hold values from -8 to 8
- text_len: int32 [4], P('req'), may hold values from 256 to 512, as said below
- hidden_state: bfloat16 [4, 64, 64, 3072], P('req', 'tile', 'col'), may hold values from -3 to 3
- modulation: float32 [28, 4, 3, 3072], P(None, 'req'), may hold values from 0.1 to 1.9
- w_attn_out: bfloat16 [1536, 3072], replicated, may hold values from -0.15625 to 0.15625
- w_final: bfloat16 [3072, 64], replicated, may hold values from -0.109375 to 0.109375
- latent: float32 [4, 64, 64, 64], P('req', 'tile', 'col'), may hold values from -6 to 6
- sigmas: float32 [29], replicated, may hold values from -1 to 3, as said below
- step_index: int32 [1], replicated, may hold values from 0 to 27
- w_preview: float32 [3, 3, 64, 64], replicated, may hold values from -0.25 to 0.25
Outputs:
- velocity: float32 [4, 64, 64, 64], P('req', 'tile', 'col')
- latent_next: float32 [4, 64, 64, 64], P('req', 'tile', 'col')
- preview: float32 [4, 64, 64, 64], P('req', 'tile', 'col')
Inputs may be any that keep to these rules, and one draw needn't show every extreme that they name: `text_len`: some request has exactly 512 live text tokens. sigmas[i] - sigmas[i + 1] lies between 0.1 / 28 and 3.4 / 28.
All inputs are finite; a program needn't handle non-finite values.
Results may differ from a plain program's by a relative error of at most 0.005.
Values may be sent and summed in bfloat16 or wider, within the bound.
A program may use at most 320 MiB of HBM per device.

v0:
```python
import math
import jax
import jax.numpy as jnp
from jax import lax
from jax.sharding import PartitionSpec as P

HD = 128
norm_eps = 1e-06


def padded_2(cells, sides, width):
    for axis, dim in sides:
        count = lax.axis_size(axis)
        ends = count - 1
        head = lax.slice_in_dim(cells, 0, width, axis=dim)
        tail = lax.slice_in_dim(cells, cells.shape[dim] - width, cells.shape[dim], axis=dim)
        cells = jnp.concatenate(
            [
                lax.ppermute(tail, axis, [(i, (i + 1) % count) for i in range(ends)]),
                cells,
                lax.ppermute(head, axis, [((i + 1) % count, i) for i in range(ends)]),
            ],
            axis=dim,
        )
    return cells


def make_fold(queries, img_rows, text_rows, text_limit):
    score_scale = 1.0 / math.sqrt(HD)
    shard_rows = img_rows + text_rows

    def fold_step(carry, piece, start):
        run_max, run_sum, run_acc = carry
        piece_len = piece.shape[0]
        key_index = jnp.arange(piece_len, dtype=jnp.int32)
        in_shard = key_index % shard_rows
        text_pos = key_index // shard_rows * text_rows + in_shard - img_rows
        key_live = (in_shard < img_rows) | (text_pos < text_limit)
        scores = (
            jnp.einsum("qhd,khd->hqk", queries, piece[:, 0], preferred_element_type=jnp.float32)
            * score_scale
        )
        scores = jnp.where(key_live[None, None, :], scores, -1e30)
        new_max = jnp.maximum(run_max, jnp.max(scores, axis=2))
        weights = jnp.where(key_live[None, None, :], jnp.exp(scores - new_max[:, :, None]), 0.0)
        run_sum = jnp.sum(weights, axis=2)
        run_acc = jnp.einsum(
            "hqk,khd->hqd",
            weights.astype(jnp.bfloat16),
            piece[:, 1],
            preferred_element_type=jnp.float32,
        )
        return (new_max, run_sum, run_acc)

    return fold_step


def start_carry(query_rows, head_count):
    return (
        jnp.full((head_count, query_rows), -1e30, jnp.float32),
        jnp.zeros((head_count, query_rows), jnp.float32),
        jnp.zeros((head_count, query_rows, HD), jnp.float32),
    )


def finish(carry):
    run_max, run_sum, run_acc = carry
    return jnp.transpose(run_acc / run_sum[:, :, None], (1, 0, 2)).astype(jnp.bfloat16)


def body(
    img_qkv,
    txt_kv,
    text_len,
    hidden_state,
    modulation,
    w_attn_out,
    w_final,
    latent,
    sigmas,
    step_index,
    w_preview,
):
    tile_rows = img_qkv.shape[1]
    grid_cols = img_qkv.shape[2]
    local_heads = img_qkv.shape[4] // HD
    text_rows = txt_kv.shape[1]
    tile_cols = hidden_state.shape[2]
    col_count = grid_cols // tile_cols
    own_rows = tile_rows * tile_cols
    text_limit = text_len[0]
    all_heads = local_heads * col_count
    img_block = img_qkv[0].reshape(tile_rows, grid_cols, 3, local_heads, HD)
    txt_block = txt_kv[0].reshape(1, text_rows, 2, local_heads, HD)
    img_mixed, txt_mixed = (
        lax.all_to_all(img_block, "col", split_axis=1, concat_axis=3, tiled=True),
        lax.all_to_all(txt_block, "col", split_axis=1, concat_axis=3, tiled=True),
    )
    img_flat = img_mixed.reshape(own_rows, 3, all_heads, HD)
    txt_flat = txt_mixed.reshape(text_rows // col_count, 2, all_heads, HD)
    key_value = jnp.concatenate([img_flat[:, 1:], txt_flat], axis=0)
    fold_step = make_fold(img_flat[:, 0], own_rows, text_rows // col_count, text_limit)
    carry = fold_step(
        start_carry(own_rows, all_heads),
        lax.all_gather(key_value, ("tile", "col"), axis=0, tiled=True),
        jnp.int32(0),
    )
    attended = finish(carry).reshape(own_rows, all_heads * HD)
    branch = jnp.dot(attended, w_attn_out, preferred_element_type=jnp.float32)
    step_now = step_index[0]
    mod_now = lax.dynamic_index_in_dim(modulation, step_now, 0, keepdims=False)[0]
    width = hidden_state.shape[3]
    mixed_state = (
        hidden_state[0].reshape(own_rows, width).astype(jnp.float32) + mod_now[0][None, :] * branch
    )
    row_mean = jnp.mean(mixed_state, axis=1, keepdims=True)
    centred = mixed_state - row_mean
    row_var = jnp.mean(centred * centred, axis=1, keepdims=True)
    normed = (
        centred / jnp.sqrt(row_var + norm_eps) * (1.0 + mod_now[2][None, :]) + mod_now[1][None, :]
    )
    normed = normed.astype(jnp.bfloat16)
    velocity = jnp.dot(normed, w_final, preferred_element_type=jnp.float32)
    channels = velocity.shape[1]
    sigma_step = sigmas[step_now + 1] - sigmas[step_now]
    updated = latent[0].reshape(own_rows, channels) + sigma_step * velocity
    grid_field = updated.reshape(tile_rows, tile_cols, channels)
    padded = padded_2(grid_field, (("tile", 0), ("col", 1)), 1)
    preview = jnp.zeros((tile_rows, tile_cols, channels), jnp.float32)
    for row_off in range(3):
        for col_off in range(3):
            preview = preview + jnp.einsum(
                "yxc,cd->yxd",
                padded[row_off : row_off + tile_rows, col_off : col_off + tile_cols],
                w_preview[row_off, col_off],
                precision=lax.Precision.HIGHEST,
            )
    return (velocity.reshape(1, tile_rows, tile_cols, channels), grid_field[None], preview[None])


def solution(mesh):
    placed = (
        P("req", "tile", None, None, "col"),
        P("req", "tile", None, "col"),
        P("req"),
        P("req", "tile", "col", None),
        P(None, "req", None, None),
        P(),
        P(),
        P("req", "tile", "col", None),
        P(),
        P(),
        P(),
    )
    return jax.shard_map(
        body,
        mesh=mesh,
        in_specs=placed,
        out_specs=(
            P("req", "tile", "col", None),
            P("req", "tile", "col", None),
            P("req", "tile", "col", None),
        ),
        check_vma=False,
    )
```

profile of v0, /device:TPU:0, one launch (start us, length us, event | category | flops | bytes accessed | tf_op | source)
XLA Modules:
  0.0 456.4 jit_solution(9621636207864728363)
XLA Ops:
  7.2 0.0 copy-start
  7.2 10.8 %reshape_squeeze.10 = bf16[16,64,3,6,128]{4,3,1,2,0:T(8,128)(2,1)} reshape(bf16[1,16,64,3,768]{4,2,3,1,0:T(8,128)(2,1)} %param.11) | data formatting | bytes 9437184 | tf_op jit(solution)/shard_map/reshape;squeeze | solution.py:93
  18.0 10.5 %copy.59 = bf16[16,64,3,6,128]{4,0,3,2,1:T(8,128)(2,1)} copy(bf16[16,64,3,6,128]{4,3,1,2,0:T(8,128)(2,1)} %reshape_squeeze.10) | data formatting | bytes 9437184 | tf_op jit(solution)/shard_map/reshape;squeeze | solution.py:93
  28.5 0.0 copy-start.3
  28.5 5.9 %all-to-all-start = ((bf16[16,64,3,6,128]{4,0,3,2,1:T(8,128)(2,1)}), bf16[16,64,3,6,128]{4,0,3,2,1:T(8,128)(2,1)}, u32[]{:S(2)}, u32[]{:S(2)}) async-start(bf16[16,64,3,6,128]{4,0,3,2,1:T(8,128)(2,1)} %copy.59), calls=%async_computation | async-start | bytes 9437184 | tf_op jit(solution)/shard_map/all_to_all | solution.py:96
  34.4 0.0 copy-done.3
  34.4 0.5 copy.62
  34.9 1.1 copy.63
  36.0 3.3 all-to-all-done
  39.2 4.2 all-to-all-start.1
  43.4 0.0 all-gather.2.cloned.1.call-start
  43.5 4.2 copy.61
  47.6 0.0 copy-start.1
  47.6 2.1 copy-done.1
  49.8 0.3 slice.131
  50.1 0.0 copy-start.5
  50.1 0.0 all-to-all-done.1
  50.1 1.1 copy.64
  51.2 2.0 pad_maximum_fusion
  53.2 0.0 all-gather.2.cloned.1.call-update
  54.6 1.1 copy.69
  55.7 0.0 copy-done.5
  55.7 0.6 fusion.73
  57.6 0.8 dynamic-slice_add_fusion
  58.4 243.5 %all-gather.2.cloned.1.call-done = bf16[4608,2,12,128]{3,0,2,1:T(8,128)(2,1)} async-done(((bf16[576,2,12,128]{3,0,2,1:T(8,128)(2,1)}), bf16[4608,2,12,128]{3,0,2,1:T(8,128)(2,1)}) %all-gather.2.cloned.1.call-update) | async-done | bytes 28311568 | tf_op jit(solution)/shard_map/all_gather | solution.py:105
  301.9 43.7 %bitcast_reduce_fusion = (f32[12,512]{1,0:T(8,128)S(1)}, f32[12,4608,512]{2,1,0:T(8,128)}) fusion(pred[4608]{0:T(1024)(128)(4,1)S(1)} %fusion.67, bf16[512,3,12,128]{3,0,2,1:T(8,128)(2,1)} %bitcast.136, bf16[4608,2,12,128]{3,0,2,1:T(8,128)(2,1)} %all-gather.2.cloned.1.call-done), kind=kOutput, calls=%fused_computation.1 | convolution fusion | flops 7332685824 | bytes 129004032 | tf_op jit(solution)/shard_map/qhd,khd->hqk/dot_general | solution.py:40
  345.6 35.4 %fusion.2 = f32[12,512]{1,0:T(8,128)S(1)} fusion(f32[12,4608,512]{2,1,0:T(8,128)} %get-tuple-element.18, f32[12,512]{1,0:T(8,128)S(1)} %broadcast_maximum_fusion, pred[4608]{0:T(1024)(128)(4,1)S(1)} %fusion.67), kind=kLoop, calls=%fused_computation.5 | loop fusion | flops 141551616 | bytes 113299968 | tf_op jit(solution)/shard_map/reduce_sum | solution.py:46
  381.0 42.5 %fusion.9 = bf16[512,12,128]{0,2,1:T(8,128)(2,1)S(1)} fusion(bf16[4608,2,12,128]{3,0,2,1:T(8,128)(2,1)} %all-gather.2.cloned.1.call-done, f32[12,4608,512]{2,1,0:T(8,128)} %get-tuple-element.18, f32[12,512]{1,0:T(8,128)S(1)} %broadcast_maximum_fusion, pred[4608]{0:T(1024)(128)(4,1)S(1)} %fusion.67, f32[512,12]{0,1:T(8,128)S(1)} %bitcast.148), kind=kOutput, calls=%fused_computation.18 | convolution fusion | flops 7390887936 | bytes 129050624 | tf_op jit(solution)/shard_map/hqk,khd->hqd/dot_general | solution.py:47
  423.5 9.1 %fusion.74 = (f32[512]{0:T(512)S(1)}, f32[512,3072]{1,0:T(8,128)S(1)}) fusion(bf16[512,1536]{0,1:T(8,128)(2,1)S(1)} %bitcast.153, bf16[1536,3072]{1,0:T(8,128)(2,1)} %param.16, f32[3072]{0:T(1024)S(1)} %bitcast.151, bf16[512,3072]{1,0:T(8,128)(2,1)} %bitcast.152), kind=kOutput, calls=%fused_computation.103 | convolution fusion | flops 4838129152 | bytes 20461568 | tf_op jit(solution)/shard_map/dot_general | solution.py:109
  432.6 0.8 multiply_reduce_fusion
  433.3 0.0 copy-done
  433.3 0.0 copy-start.4
  433.3 1.4 multiply_add_fusion
  434.8 0.1 copy.70
  434.9 0.0 copy-start.2
  434.9 0.1 slice_bitcast_fusion.9
  435.0 1.3 collective-permute-start
  436.3 1.3 collective-permute-start.1
  437.6 0.0 copy-done.4
  437.6 0.4 fusion.42
  438.0 0.8 copy.68
  438.8 0.0 collective-permute-done
  438.8 0.1 copy.72
  438.9 0.4 fusion.20
  439.2 2.9 collective-permute-done.1
  442.1 0.1 copy.73
  442.2 1.3 collective-permute-start.2
  443.5 1.3 collective-permute-start.3
  444.8 0.4 fusion.24
  445.2 0.0 collective-permute-done.2
  445.2 1.4 collective-permute-done.3
  446.6 0.1 maximum_maximum_fusion
  446.6 0.3 fusion.35
  447.0 0.4 fusion.28
  447.3 0.4 fusion.33
  447.7 0.4 fusion.30
  448.1 0.4 fusion.17
  448.5 1.1 fusion.19
  449.5 0.0 copy-done.2
  (6 shorter events, 0.1 us)
Async XLA Ops:
  7.2 426.2 %copy-start = (bf16[3072,64]{0,1:T(8,128)(2,1)S(1)}, bf16[3072,64]{0,1:T(8,128)(2,1)}, u32[]{:S(2)}) copy-start(bf16[3072,64]{0,1:T(8,128)(2,1)} %param.17) | copy-start | bytes 1179652
  28.5 5.9 %copy-start.3 = (bf16[1,128,2,768]{3,2,1,0:T(2,128)(2,1)S(1)}, bf16[1,128,2,768]{3,2,1,0:T(2,128)(2,1)}, u32[]{:S(2)}) copy-start(bf16[1,128,2,768]{3,2,1,0:T(2,128)(2,1)} %param.12) | copy-start | bytes 1179652
  28.5 10.8 %all-to-all-start = ((bf16[16,64,3,6,128]{4,0,3,2,1:T(8,128)(2,1)}), bf16[16,64,3,6,128]{4,0,3,2,1:T(8,128)(2,1)}, u32[]{:S(2)}, u32[]{:S(2)}) async-start(bf16[16,64,3,6,128]{4,0,3,2,1:T(8,128)(2,1)} %copy.59), calls=%async_computation | async-start | bytes 9437184 | tf_op jit(solution)/shard_map/all_to_all | solution.py:96
  39.2 10.8 %all-to-all-start.1 = ((bf16[1,128,2,6,128]{4,2,3,0,1:T(2,128)(2,1)}), bf16[1,128,2,6,128]{4,2,3,0,1:T(2,128)(2,1)}, u32[]{:S(2)}, u32[]{:S(2)}) async-start(bf16[1,128,2,6,128]{4,2,3,0,1:T(2,128)(2,1)} %copy.63), calls=%async_computation.1 | async-start | bytes 786432 | tf_op jit(solution)/shard_map/all_to_all | solution.py:97
  43.4 258.5 %all-gather.2.cloned.1.call-start = ((), (), s32[]{:S(2)}) async-start(), calls=%async_computation.2 | async-start | bytes 31850496 | tf_op jit(solution)/shard_map/all_gather | solution.py:105
  47.6 2.1 copy-start.1
  50.1 5.6 %copy-start.5 = (f32[29]{0:T(128)S(1)}, f32[29]{0:T(128)}, u32[]{:S(2)}) copy-start(f32[29]{0:T(128)} %param.19) | copy-start | bytes 352
  433.3 4.3 copy-start.4
  434.9 14.6 %copy-start.2 = (f32[512,64]{1,0:T(8,128)}, f32[512,64]{1,0:T(8,128)S(1)}, u32[]{:S(2)}) copy-start(f32[512,64]{1,0:T(8,128)S(1)} %copy.70) | copy-start | bytes 393220
  435.0 3.8 collective-permute-start
  436.3 5.8 %collective-permute-start.1 = (f32[1,32,64]{1,2,0:T(8,128)S(1)}, f32[1,32,64]{1,2,0:T(8,128)S(1)}, u32[]{:S(2)}, u32[]{:S(2)}) collective-permute-start(f32[1,32,64]{1,2,0:T(8,128)S(1)} %get-tuple-element.14), channel_id=1, source_target_pairs={{2,0},{4,2},{6,4},{3,1},{5,3},{7,5},{10,8},{12,10},{14,12},{11,9},... | collective-permute-start | bytes 24584 | tf_op jit(solution)/shard_map/ppermute | solution.py:21
  442.2 3.0 collective-permute-start.2
  443.5 3.1 collective-permute-start.3
Sparse Core Ops, SparseCore 0:
  53.4 248.4 all-gather.1
where the time goes:
time: 457 us; the launch traced here: 456 us
  waiting for transfers between devices  251 us (55%)
  matrix products  101 us (22%)
  other arithmetic  39.1 us (9%)
  local copies, waits for them, and re-layouts  33.4 us (7%)
  between operations  17 us (4%)
  starting transfers between devices  15.3 us (3%)
    all_gather x1, waiting for transfers between devices, body(): lax.all_gather(key_value, ('tile', 'col'), axis=0, tiled=True)  244 us
    dot_general x1, matrix products, fold_step(): jnp.einsum('qhd,khd->hqk', queries, piece[:, 0], preferred_element_type=j...  43.7 us
    dot_general x1, matrix products, fold_step(): jnp.einsum('hqk,khd->hqd', weights.astype(jnp.bfloat16), piece[:, 1], pre...  42.5 us
    reduce_sum x1, other arithmetic, fold_step(): run_sum = jnp.sum(weights, axis=2)  35.4 us
    another operation x2, local copies, waits for them, and re-layouts, body(): img_block = img_qkv[0].reshape(tile_rows, grid_cols, 3, local_heads, HD)  21.3 us
  transfers between devices with their start and end apart: 7, of which 4 were waited for; matrix products, arithmetic and copies ran while one was open for 2% of the time, Pallas kernels for 0%

commit v1 on v0

--- a/solution.py
+++ b/solution.py
@@ -6,6 +6,24 @@
 
 HD = 128
 norm_eps = 1e-06
+
+
+def gather_around(array, axis, dim):
+    ways, here, lap = (lax.axis_size(axis), lax.axis_index(axis), array.shape[dim])
+    lengths = [n * ways if d == dim else n for d, n in enumerate(array.shape)]
+    full = lax.dynamic_update_slice_in_dim(
+        jnp.zeros(lengths, array.dtype), array, here * lap, axis=dim
+    )
+    going_up = going_down = array
+    for far in range(1, ways // 2 + 1):
+        going_up = lax.ppermute(going_up, axis, [(d, (d + 1) % ways) for d in range(ways)])
+        full = lax.dynamic_update_slice_in_dim(full, going_up, (here - far) % ways * lap, axis=dim)
+        if 2 * far < ways:
+            going_down = lax.ppermute(going_down, axis, [(d, (d - 1) % ways) for d in range(ways)])
+            full = lax.dynamic_update_slice_in_dim(
+                full, going_down, (here + far) % ways * lap, axis=dim
+            )
+    return full
 
 
 def padded_2(cells, sides, width):
@@ -101,9 +119,7 @@
     key_value = jnp.concatenate([img_flat[:, 1:], txt_flat], axis=0)
     fold_step = make_fold(img_flat[:, 0], own_rows, text_rows // col_count, text_limit)
     carry = fold_step(
-        start_carry(own_rows, all_heads),
-        lax.all_gather(key_value, ("tile", "col"), axis=0, tiled=True),
-        jnp.int32(0),
+        start_carry(own_rows, all_heads), gather_around(key_value, ("tile", "col"), 0), jnp.int32(0)
     )
     attended = finish(carry).reshape(own_rows, all_heads * HD)
     branch = jnp.dot(attended, w_attn_out, preferred_element_type=jnp.float32)

time: 457 us -> 494 us (1.081)
  local copies, waits for them, and re-layouts: 33.4 us -> 74.9 us
  between operations: 17 us -> 4.47 us
  starting transfers between devices: 15.3 us -> 27.3 us
  waiting for transfers between devices: 251 us -> 246 us
    all_gather x1 -> x0, waiting for transfers between devices: 244 us -> none  [body(): lax.all_gather(key_value, ('tile', 'col'), axis=0, tiled=True)]
    ppermute x0 -> x7, waiting for transfers between devices: none -> 237 us  [the longest x4 237 us: gather_around(): lax.ppermute(going_up, axis, [(d, (d + 1) % ways) for d in range(ways)])]
    dynamic_update_slice x0 -> x7, local copies, waits for them, and re-layouts: none -> 27 us  [the longest x4 15.7 us: gather_around(): lax.dynamic_update_slice_in_dim(full, going_up, (here - far) % ways * lap...]
    ppermute x0 -> x7, starting transfers between devices: none -> 10.4 us  [the longest x3 9.97 us: gather_around(): lax.ppermute(going_down, axis, [(d, (d - 1) % ways) for d in range(ways)])]
    broadcast_in_dim x0 -> x1, local copies, waits for them, and re-layouts: none -> 9.49 us  [gather_around(): jnp.zeros(lengths, array.dtype)]
  transfers between devices with their start and end apart: 7 -> 13, of which waited for: 4 -> 7; matrix products, arithmetic and copies ran while one was open for 2% -> 7% of each run, Pallas kernels for 0% -> 0%
where the time goes in v1:
time: 494 us
  waiting for transfers between devices  246 us (50%)
  matrix products  101 us (20%)
  local copies, waits for them, and re-layouts  74.9 us (15%)
  other arithmetic  40.5 us (8%)
  starting transfers between devices  27.3 us (6%)
    ppermute x4, waiting for transfers between devices, gather_around(): lax.ppermute(going_up, axis, [(d, (d + 1) % ways) for d in range(ways)])  237 us
    dot_general x1, matrix products, fold_step(): jnp.einsum('qhd,khd->hqk', queries, piece[:, 0], preferred_element_type=j...  43.7 us
    dot_general x1, matrix products, fold_step(): jnp.einsum('hqk,khd->hqd', weights.astype(jnp.bfloat16), piece[:, 1], pre...  42.6 us
    reduce_sum x1, other arithmetic, fold_step(): run_sum = jnp.sum(weights, axis=2)  35.4 us
    another operation x2, local copies, waits for them, and re-layouts, body(): img_block = img_qkv[0].reshape(tile_rows, grid_cols, 3, local_heads, HD)  21.4 us
    dynamic_update_slice x4, local copies, waits for them, and re-layouts, gather_around(): lax.dynamic_update_slice_in_dim(full, going_up, (here - far) % ways * lap...  15.7 us
    dynamic_update_slice x3, local copies, waits for them, and re-layouts, gather_around(): lax.dynamic_update_slice_in_dim(full, going_down, (here + far) % ways * l...  11.3 us
    ppermute x3, starting transfers between devices, gather_around(): lax.ppermute(going_down, axis, [(d, (d - 1) % ways) for d in range(ways)])  9.97 us
  transfers between devices with their start and end apart: 13, of which 7 were waited for; matrix products, arithmetic and copies ran while one was open for 7% of the time, Pallas kernels for 0%

profile of v1, /device:TPU:0, one launch (start us, length us, event | category | flops | bytes accessed | tf_op | source)
XLA Modules:
  0.0 493.5 jit_solution(17110702152974670532)
XLA Ops:
  0.6 0.0 copy-start
  0.6 10.8 %reshape_squeeze.10 = bf16[16,64,3,6,128]{4,3,1,2,0:T(8,128)(2,1)} reshape(bf16[1,16,64,3,768]{4,2,3,1,0:T(8,128)(2,1)} %param.11) | data formatting | bytes 9437184 | tf_op jit(solution)/shard_map/reshape;squeeze | solution.py:111
  11.5 10.5 %copy.59 = bf16[16,64,3,6,128]{4,0,3,2,1:T(8,128)(2,1)} copy(bf16[16,64,3,6,128]{4,3,1,2,0:T(8,128)(2,1)} %reshape_squeeze.10) | data formatting | bytes 9437184 | tf_op jit(solution)/shard_map/reshape;squeeze | solution.py:111
  22.0 5.8 %all-to-all-start = ((bf16[16,64,3,6,128]{4,0,3,2,1:T(8,128)(2,1)}), bf16[16,64,3,6,128]{4,0,3,2,1:T(8,128)(2,1)}, u32[]{:S(2)}, u32[]{:S(2)}) async-start(bf16[16,64,3,6,128]{4,0,3,2,1:T(8,128)(2,1)} %copy.59), calls=%async_computation | async-start | bytes 9437184 | tf_op jit(solution)/shard_map/all_to_all | solution.py:114
  27.8 0.5 copy.62
  28.3 1.1 copy.63
  29.4 3.3 all-to-all-done
  32.7 4.2 all-to-all-start.1
  36.8 4.2 copy.61
  41.0 2.1 copy-done.1
  43.2 0.3 slice.131
  43.5 1.1 copy.64
  44.5 0.8 copy.65
  45.3 9.5 %broadcast_in_dim.37 = bf16[4608,2,12,128]{3,0,2,1:T(8,128)(2,1)} broadcast(bf16[]{:T(256)} %constant.94.clone.1), dimensions={} | broadcast | bytes 28311554 | tf_op jit(solution)/shard_map/broadcast_in_dim | solution.py:15
  54.8 2.9 pad_maximum_fusion
  57.7 0.5 collective-permute-start
  58.2 4.6 collective-permute-start.1
  62.8 75.0 %collective-permute-done = bf16[576,2,12,128]{3,0,2,1:T(8,128)(2,1)S(1)} collective-permute-done((bf16[576,2,12,128]{3,0,2,1:T(8,128)(2,1)S(1)}, bf16[576,2,12,128]{3,0,2,1:T(8,128)(2,1)S(1)}, u32[]{:S(2)}, u32[]{:S(2)}) %collective-permute-start) | collective-permute-done | bytes 3538976 | tf_op jit(solution)/shard_map/ppermute | solution.py:19
  137.9 1.8 copy-done.3
  139.6 3.5 collective-permute-start.3
  143.2 74.8 %collective-permute-done.2 = bf16[576,2,12,128]{3,0,2,1:T(8,128)(2,1)S(1)} collective-permute-done((bf16[576,2,12,128]{3,0,2,1:T(8,128)(2,1)S(1)}, bf16[576,2,12,128]{3,0,2,1:T(8,128)(2,1)S(1)}, u32[]{:S(2)}, u32[]{:S(2)}) %collective-permute-start.2) | collective-permute-done | bytes 3538976 | tf_op jit(solution)/shard_map/ppermute | solution.py:19
  218.0 1.7 copy-done.6
  219.7 1.8 collective-permute-start.5
  221.5 74.1 %collective-permute-done.4 = bf16[576,2,12,128]{3,0,2,1:T(8,128)(2,1)} collective-permute-done((bf16[576,2,12,128]{3,0,2,1:T(8,128)(2,1)S(1)}, bf16[576,2,12,128]{3,0,2,1:T(8,128)(2,1)}, u32[]{:S(2)}, u32[]{:S(2)}) %collective-permute-start.4) | collective-permute-done | bytes 3538976 | tf_op jit(solution)/shard_map/ppermute | solution.py:19
  297.0 1.7 copy.69
  298.7 0.6 fusion.73
  301.5 1.4 dynamic-slice_add_fusion
  302.8 4.4 constant_dynamic-update-slice_fusion.6
  307.2 2.4 constant_dynamic-update-slice_fusion.5
  309.6 2.4 constant_dynamic-update-slice_fusion.4
  312.0 4.5 constant_dynamic-update-slice_fusion.3
  316.5 4.4 constant_dynamic-update-slice_fusion.2
  320.9 4.4 constant_dynamic-update-slice_fusion.1
  325.4 13.3 %collective-permute-done.6 = bf16[576,2,12,128]{3,0,2,1:T(8,128)(2,1)} collective-permute-done((bf16[576,2,12,128]{3,0,2,1:T(8,128)(2,1)}, bf16[576,2,12,128]{3,0,2,1:T(8,128)(2,1)}, u32[]{:S(2)}, u32[]{:S(2)}) %collective-permute-start.6) | collective-permute-done | bytes 3538976 | tf_op jit(solution)/shard_map/ppermute | solution.py:19
  338.7 4.4 constant_dynamic-update-slice_fusion
  343.1 43.7 %bitcast_reduce_fusion = (f32[12,512]{1,0:T(8,128)S(1)}, f32[12,4608,512]{2,1,0:T(8,128)}) fusion(pred[4608]{0:T(1024)(128)(4,1)S(1)} %fusion.65, bf16[512,3,12,128]{3,0,2,1:T(8,128)(2,1)} %bitcast.136, bf16[4608,2,12,128]{3,0,2,1:T(8,128)(2,1)} %constant_dynamic-update-slice_fusion), kind=kOutput, calls=%fused_computation.1 | convolution fusion | flops 7332685824 | bytes 129004032 | tf_op jit(solution)/shard_map/qhd,khd->hqk/dot_general | solution.py:58
  386.8 35.4 %fusion.2 = f32[12,512]{1,0:T(8,128)S(1)} fusion(f32[12,4608,512]{2,1,0:T(8,128)} %get-tuple-element.20, f32[12,512]{1,0:T(8,128)S(1)} %broadcast_maximum_fusion, pred[4608]{0:T(1024)(128)(4,1)S(1)} %fusion.65), kind=kLoop, calls=%fused_computation.5 | loop fusion | flops 141551616 | bytes 113299968 | tf_op jit(solution)/shard_map/reduce_sum | solution.py:64
  422.2 42.6 %fusion.9 = bf16[512,12,128]{0,2,1:T(8,128)(2,1)S(1)} fusion(f32[512,12]{0,1:T(8,128)S(1)} %bitcast.148, bf16[4608,2,12,128]{3,0,2,1:T(8,128)(2,1)} %constant_dynamic-update-slice_fusion, f32[12,4608,512]{2,1,0:T(8,128)} %get-tuple-element.20, f32[12,512]{1,0:T(8,128)S(1)} %broadcast_maximum_fusion, pred[4608]{0:T(1024)(128)(4,1)S(1)} %fusion.65), kind=kOutput, calls=%fused_computation.18 | convolution fusion | flops 7390887936 | bytes 129050624 | tf_op jit(solution)/shard_map/hqk,khd->hqd/dot_general | solution.py:65
  464.8 0.0 copy-start.11
  464.8 0.0 copy-start.12
  464.8 9.0 %fusion.74 = (f32[512]{0:T(512)S(1)}, f32[512,3072]{1,0:T(8,128)S(1)}) fusion(bf16[512,1536]{0,1:T(8,128)(2,1)S(1)} %bitcast.153, bf16[1536,3072]{1,0:T(8,128)(2,1)} %param.16, f32[3072]{0:T(1024)S(1)} %bitcast.151, bf16[512,3072]{1,0:T(8,128)(2,1)} %bitcast.152), kind=kOutput, calls=%fused_computation.111 | convolution fusion | flops 4838129152 | bytes 20461568 | tf_op jit(solution)/shard_map/dot_general | solution.py:125
  473.9 0.8 multiply_reduce_fusion
  474.7 1.4 multiply_add_fusion
  476.1 0.1 copy.70
  476.3 0.1 slice_bitcast_fusion.7
  476.4 1.3 collective-permute-start.7
  477.7 1.3 collective-permute-start.8
  479.0 0.4 fusion.40
  479.3 0.8 copy.68
  480.2 0.1 copy.72
  480.2 0.4 fusion.18
  480.6 4.7 collective-permute-done.8
  485.3 0.1 copy.73
  485.4 1.3 collective-permute-start.10
  486.7 3.0 collective-permute-start.9
  489.8 0.4 fusion.22
  490.1 0.4 collective-permute-done.9
  490.6 0.1 maximum_maximum_fusion
  490.6 0.4 fusion.33
  491.0 0.4 fusion.26
  491.3 0.4 fusion.31
  491.7 0.4 fusion.28
  492.1 0.4 fusion.15
  492.5 1.1 fusion.17
  (40 shorter events, 0.1 us)
Async XLA Ops:
  0.6 474.0 %copy-start = (bf16[3072,64]{0,1:T(8,128)(2,1)S(1)}, bf16[3072,64]{0,1:T(8,128)(2,1)}, u32[]{:S(2)}) copy-start(bf16[3072,64]{0,1:T(8,128)(2,1)} %param.17) | copy-start | bytes 1179652
  11.5 16.3 %copy-start.9 = (bf16[1,128,2,768]{3,2,1,0:T(2,128)(2,1)S(1)}, bf16[1,128,2,768]{3,2,1,0:T(2,128)(2,1)}, u32[]{:S(2)}) copy-start(bf16[1,128,2,768]{3,2,1,0:T(2,128)(2,1)} %param.12) | copy-start | bytes 1179652
  22.0 10.7 %all-to-all-start = ((bf16[16,64,3,6,128]{4,0,3,2,1:T(8,128)(2,1)}), bf16[16,64,3,6,128]{4,0,3,2,1:T(8,128)(2,1)}, u32[]{:S(2)}, u32[]{:S(2)}) async-start(bf16[16,64,3,6,128]{4,0,3,2,1:T(8,128)(2,1)} %copy.59), calls=%async_computation | async-start | bytes 9437184 | tf_op jit(solution)/shard_map/all_to_all | solution.py:114
  32.7 10.8 %all-to-all-start.1 = ((bf16[1,128,2,6,128]{4,2,3,0,1:T(2,128)(2,1)}), bf16[1,128,2,6,128]{4,2,3,0,1:T(2,128)(2,1)}, u32[]{:S(2)}, u32[]{:S(2)}) async-start(bf16[1,128,2,6,128]{4,2,3,0,1:T(2,128)(2,1)} %copy.63), calls=%async_computation.1 | async-start | bytes 786432 | tf_op jit(solution)/shard_map/all_to_all | solution.py:115
  41.0 2.1 copy-start.1
  45.3 9.5 %copy-start.8 = (bf16[1,64,2,2,6,128]{5,1,4,3,2,0:T(8,128)(2,1)S(1)}, bf16[1,64,2,2,6,128]{5,1,4,3,2,0:T(8,128)(2,1)}, u32[]{:S(2)}) copy-start(bf16[1,64,2,2,6,128]{5,1,4,3,2,0:T(8,128)(2,1)} %copy.65) | copy-start | bytes 1179652
  54.8 243.9 %copy-start.15 = (f32[29]{0:T(128)S(1)}, f32[29]{0:T(128)}, u32[]{:S(2)}) copy-start(f32[29]{0:T(128)} %param.19) | copy-start | bytes 352
  57.7 80.1 %collective-permute-start = (bf16[576,2,12,128]{3,0,2,1:T(8,128)(2,1)S(1)}, bf16[576,2,12,128]{3,0,2,1:T(8,128)(2,1)S(1)}, u32[]{:S(2)}, u32[]{:S(2)}) collective-permute-start(bf16[576,2,12,128]{3,0,2,1:T(8,128)(2,1)S(1)} %get-tuple-element.6), channel_id=1, source_target_pairs={{0,1},{1,2},{2,3},{3,4},{4,5},{5,6},{6,7},{7,0},{8,9},{9,10},{10,1... | collective-permute-start | bytes 10616840 | tf_op jit(solution)/shard_map/ppermute | solution.py:19
  58.2 81.4 %collective-permute-start.1 = (bf16[576,2,12,128]{3,0,2,1:T(8,128)(2,1)S(1)}, bf16[576,2,12,128]{3,0,2,1:T(8,128)(2,1)S(1)}, u32[]{:S(2)}, u32[]{:S(2)}) collective-permute-start(bf16[576,2,12,128]{3,0,2,1:T(8,128)(2,1)S(1)} %get-tuple-element.6), channel_id=1, source_target_pairs={{0,7},{1,0},{2,1},{3,2},{4,3},{5,4},{6,5},{7,6},{8,15},{9,8},{10,9... | collective-permute-start | bytes 10616840 | tf_op jit(solution)/shard_map/ppermute | solution.py:22
  137.9 1.8 copy-start.3
  139.6 78.3 %collective-permute-start.2 = (bf16[576,2,12,128]{3,0,2,1:T(8,128)(2,1)S(1)}, bf16[576,2,12,128]{3,0,2,1:T(8,128)(2,1)S(1)}, u32[]{:S(2)}, u32[]{:S(2)}) collective-permute-start(bf16[576,2,12,128]{3,0,2,1:T(8,128)(2,1)S(1)} %collective-permute-done), channel_id=1, source_target_pairs={{0,1},{1,2},{2,3},{3,4},{4,5},{5,6},{6,7},{7,0},{8,9},{9,10},{10,1... | collective-permute-start | bytes 10616840 | tf_op jit(solution)/shard_map/ppermute | solution.py:19
  139.6 78.3 %copy-start.4 = (bf16[576,2,12,128]{3,0,2,1:T(8,128)(2,1)}, bf16[576,2,12,128]{3,0,2,1:T(8,128)(2,1)S(1)}, u32[]{:S(2)}) copy-start(bf16[576,2,12,128]{3,0,2,1:T(8,128)(2,1)S(1)} %collective-permute-done.1) | copy-start | bytes 10616836
  139.6 78.3 %collective-permute-start.3 = (bf16[576,2,12,128]{3,0,2,1:T(8,128)(2,1)S(1)}, bf16[576,2,12,128]{3,0,2,1:T(8,128)(2,1)}, u32[]{:S(2)}, u32[]{:S(2)}) collective-permute-start(bf16[576,2,12,128]{3,0,2,1:T(8,128)(2,1)S(1)} %collective-permute-done.1), channel_id=1, source_target_pairs={{0,7},{1,0},{2,1},{3,2},{4,3},{5,4},{6,5},{7,6},{8,15},{9,8},{10,9... | collective-permute-start | bytes 10616840 | tf_op jit(solution)/shard_map/ppermute | solution.py:22
  218.0 1.8 copy-start.6
  218.0 77.7 %collective-permute-start.4 = (bf16[576,2,12,128]{3,0,2,1:T(8,128)(2,1)S(1)}, bf16[576,2,12,128]{3,0,2,1:T(8,128)(2,1)}, u32[]{:S(2)}, u32[]{:S(2)}) collective-permute-start(bf16[576,2,12,128]{3,0,2,1:T(8,128)(2,1)S(1)} %collective-permute-done.2), channel_id=1, source_target_pairs={{0,1},{1,2},{2,3},{3,4},{4,5},{5,6},{6,7},{7,0},{8,9},{9,10},{10,1... | collective-permute-start | bytes 10616840 | tf_op jit(solution)/shard_map/ppermute | solution.py:19
  219.7 101.2 %collective-permute-start.5 = (bf16[576,2,12,128]{3,0,2,1:T(8,128)(2,1)}, bf16[576,2,12,128]{3,0,2,1:T(8,128)(2,1)}, u32[]{:S(2)}, u32[]{:S(2)}) collective-permute-start(bf16[576,2,12,128]{3,0,2,1:T(8,128)(2,1)} %collective-permute-done.3), channel_id=1, source_target_pairs={{0,7},{1,0},{2,1},{3,2},{4,3},{5,4},{6,5},{7,6},{8,15},{9,8},{10,9... | collective-permute-start | bytes 10616840 | tf_op jit(solution)/shard_map/ppermute | solution.py:22
  295.7 43.0 %collective-permute-start.6 = (bf16[576,2,12,128]{3,0,2,1:T(8,128)(2,1)}, bf16[576,2,12,128]{3,0,2,1:T(8,128)(2,1)}, u32[]{:S(2)}, u32[]{:S(2)}) collective-permute-start(bf16[576,2,12,128]{3,0,2,1:T(8,128)(2,1)} %collective-permute-done.4), channel_id=1, source_target_pairs={{0,1},{1,2},{2,3},{3,4},{4,5},{5,6},{6,7},{7,0},{8,9},{9,10},{10,1... | collective-permute-start | bytes 10616840 | tf_op jit(solution)/shard_map/ppermute | solution.py:19
  298.7 8.5 %copy-start.5 = (bf16[576,2,12,128]{3,0,2,1:T(8,128)(2,1)S(1)}, bf16[576,2,12,128]{3,0,2,1:T(8,128)(2,1)}, u32[]{:S(2)}) copy-start(bf16[576,2,12,128]{3,0,2,1:T(8,128)(2,1)} %copy-done.4) | copy-start | bytes 10616836
  298.7 10.9 %copy-start.7 = (bf16[576,2,12,128]{3,0,2,1:T(8,128)(2,1)S(1)}, bf16[576,2,12,128]{3,0,2,1:T(8,128)(2,1)}, u32[]{:S(2)}) copy-start(bf16[576,2,12,128]{3,0,2,1:T(8,128)(2,1)} %copy-done.6) | copy-start | bytes 10616836
  422.2 42.6 %copy-start.14 = (f32[1,1,1,3072]{3,1,2,0:T(1,128)S(1)}, f32[1,1,1,3072]{3,1,2,0:T(1,128)}, u32[]{:S(2)}) copy-start(f32[1,1,1,3072]{3,1,2,0:T(1,128)} %get-tuple-element.9) | copy-start | bytes 36868
  464.8 9.9 %copy-start.11 = (f32[512,64]{0,1:T(8,128)S(1)}, f32[512,64]{0,1:T(8,128)}, u32[]{:S(2)}) copy-start(f32[512,64]{0,1:T(8,128)} %copy.69) | copy-start | bytes 393220
  464.8 9.9 %copy-start.12 = (f32[1,1,1,3072]{3,1,2,0:T(1,128)S(1)}, f32[1,1,1,3072]{3,1,2,0:T(1,128)}, u32[]{:S(2)}) copy-start(f32[1,1,1,3072]{3,1,2,0:T(1,128)} %get-tuple-element.8) | copy-start | bytes 36868
  464.8 9.9 %copy-start.13 = (f32[1,1,1,3072]{3,1,2,0:T(1,128)S(1)}, f32[1,1,1,3072]{3,1,2,0:T(1,128)}, u32[]{:S(2)}) copy-start(f32[1,1,1,3072]{3,1,2,0:T(1,128)} %get-tuple-element.10) | copy-start | bytes 36868
  474.7 4.3 copy-start.10
  476.3 17.3 %copy-start.2 = (f32[512,64]{1,0:T(8,128)}, f32[512,64]{1,0:T(8,128)S(1)}, u32[]{:S(2)}) copy-start(f32[512,64]{1,0:T(8,128)S(1)} %copy.70) | copy-start | bytes 393220
  476.4 3.8 collective-permute-start.7
  477.7 7.7 %collective-permute-start.8 = (f32[1,32,64]{1,2,0:T(8,128)S(1)}, f32[1,32,64]{1,2,0:T(8,128)S(1)}, u32[]{:S(2)}, u32[]{:S(2)}) collective-permute-start(f32[1,32,64]{1,2,0:T(8,128)S(1)} %get-tuple-element.16), channel_id=1, source_target_pairs={{2,0},{4,2},{6,4},{3,1},{5,3},{7,5},{10,8},{12,10},{14,12},{11,9},... | collective-permute-start | bytes 24584 | tf_op jit(solution)/shard_map/ppermute | solution.py:39
  485.4 4.7 collective-permute-start.10
  486.7 3.8 collective-permute-start.9
